TPU v7x, 32 devices: a whole 2x2x4 slice. The times are simulated.
32 devices in a mesh: site: 8 (over y, x, core), real: 4 (over z).
Axes of the slice: x: 2, y: 2, z: 4, core: 2. Of those that a mesh axis runs over, the one named last changes fastest.
Arguments:
- field: float32 [64, 16384], P('real', 'site'), may hold values from -6 to 6
- observed: float32 [20480], P('site'), may hold values from -6 to 6
- inv_cov: float32 [20480, 20480], P('site', 'real'), may hold values from -0.0012207031 to 0.0012207031
- site_xy: float32 [2, 16384], P(None, 'site'), may hold values from 0 to 200
- station_site: int32 [20480], P('site'), may hold values from 0 to 16383, as said below
- site_mean: float32 [16384], P('site'), may hold values from -3 to 0
- building_site: int32 [32768], P('site'), may hold values from 0 to 16383, as said below
- building_class: int32 [32768], P('site'), may hold values from 0 to 35
- building_tract: int32 [32768], P('site'), may hold values from 0 to 4095
- building_value: float32 [32768], P('site')
- median_ln: float32 [4, 36], replicated, may hold values from -2.3 to 0.4
- beta_ln: float32 [36], replicated, may hold values from 0.4 to 0.8
- loss_step: float32 [4, 36], replicated, may hold values from 0.02 to 0.3
Outputs:
- cond_field: float32 [64, 16384], P('real', 'site')
- tract_loss: float32 [64, 4096], P('real', 'site')
- total_loss: float32 [64], P('real')
Inputs may be any that keep to these rules, and one draw needn't show every extreme that they name: `station_site`: the stations of rows d * 2560 to (d + 1) * 2560 - 1 stand at sites d * 2048 to (d + 1) * 2048 - 1; several stations may share a site. `building_site`: the buildings of rows d * 4096 to (d + 1) * 4096 - 1 stand at sites d * 2048 to (d + 1) * 2048 - 1.
All inputs are finite; a program needn't handle non-finite values.
Results may differ from a plain program's by a relative error of at most 0.003.
Values may be sent and summed in bfloat16 or wider, within the bound.
A program may use at most 128 MiB of HBM per device.

v0:
```python
import math
import jax
import jax.numpy as jnp
from jax import lax
from jax.sharding import PartitionSpec as P

TRACT_DEV = 512


def normal_cdf(value):
    return 0.5 * (1.0 + lax.erf(value * 0.7071067811865476))


def shards(
    field,
    observed,
    inv_cov,
    site_xy,
    station_site,
    site_mean,
    building_site,
    building_class,
    building_tract,
    building_value,
    median_ln,
    beta_ln,
    loss_step,
):
    real_rows = field.shape[0]
    site_block = field.shape[1]
    site_count = lax.axis_size("site")
    first_site = lax.axis_index("site") * site_block
    station_local = station_site - first_site
    station_field = jnp.take(field, station_local, axis=1)
    innov = observed[None, :] - station_field
    partial_w = jnp.dot(
        lax.all_gather(innov, "real", axis=0, tiled=True),
        inv_cov,
        precision=lax.Precision.HIGHEST,
        preferred_element_type=jnp.float32,
    )
    station_xy = jnp.take(site_xy, station_local, axis=1)
    block_width = math.gcd(site_block, 256)
    summed = lax.psum(partial_w, "site")
    weights = lax.all_to_all(
        summed.astype(jnp.bfloat16), "real", split_axis=0, concat_axis=1, tiled=True
    )
    piece = lax.all_gather(station_xy, "site", axis=1, tiled=True)

    def one_block(index, acc):
        anchor = index * block_width
        east = lax.dynamic_slice_in_dim(site_xy[0], anchor, block_width)
        north = lax.dynamic_slice_in_dim(site_xy[1], anchor, block_width)
        dist = jnp.sqrt(
            (east[:, None] - piece[0][None, :]) ** 2 + (north[:, None] - piece[1][None, :]) ** 2
        )
        cross = jnp.exp(-dist / 30.0).astype(jnp.bfloat16)
        term = lax.dot_general(
            weights, cross, (((1,), (1,)), ((), ())), preferred_element_type=jnp.float32
        )
        current = lax.dynamic_slice_in_dim(acc, anchor, block_width, 1)
        return lax.dynamic_update_slice_in_dim(acc, current + term, anchor, 1)

    cond_field = lax.fori_loop(0, site_block // block_width, one_block, field)
    ln_im = site_mean[None, :] + 0.6 * cond_field
    build_local = building_site - first_site
    build_im = jnp.take(ln_im, build_local, axis=1)
    class_count = median_ln.shape[1]
    class_table = (
        building_class[:, None] == jnp.arange(class_count, dtype=jnp.int32)[None, :]
    ).astype(jnp.float32)
    median_b = jnp.dot(
        median_ln,
        class_table.T,
        precision=lax.Precision.HIGHEST,
        preferred_element_type=jnp.float32,
    )
    step_b = jnp.dot(
        loss_step,
        class_table.T,
        precision=lax.Precision.HIGHEST,
        preferred_element_type=jnp.float32,
    )
    beta_b = jnp.dot(
        beta_ln[None, :],
        class_table.T,
        precision=lax.Precision.HIGHEST,
        preferred_element_type=jnp.float32,
    )
    exceed = normal_cdf((build_im[None, :, :] - median_b[:, None, :]) / beta_b[:, None, :])
    loss = building_value[None, :] * jnp.sum(exceed * step_b[:, None, :], axis=0)
    build_count = loss.shape[1]
    tract_count = TRACT_DEV * site_count
    group_width = math.gcd(build_count, 512)
    groups = build_count // group_width
    loss_groups = loss.reshape(real_rows, groups, group_width).transpose(1, 0, 2)
    tract_groups = building_tract.reshape(groups, group_width)

    def add_group(acc, pair):
        loss_part, tracts = pair
        table = (tracts[:, None] == jnp.arange(tract_count, dtype=jnp.int32)[None, :]).astype(
            jnp.float32
        )
        return (
            acc
            + jnp.dot(
                loss_part,
                table,
                precision=lax.Precision.HIGHEST,
                preferred_element_type=jnp.float32,
            ),
            None,
        )

    tract_part, _ = lax.scan(
        add_group, jnp.zeros((real_rows, tract_count), jnp.float32), (loss_groups, tract_groups)
    )
    all_buildings = build_count * site_count
    tract_loss = lax.psum_scatter(tract_part, "site", scatter_dimension=1, tiled=True)
    total_loss = lax.psum(jnp.sum(tract_loss, axis=1), "site") / all_buildings
    return (cond_field, tract_loss, total_loss)


def solution(mesh):
    placed = (
        P("real", "site"),
        P("site"),
        P("site", "real"),
        P(None, "site"),
        P("site"),
        P("site"),
        P("site"),
        P("site"),
        P("site"),
        P("site"),
        P(),
        P(),
        P(),
    )
    return jax.shard_map(
        shards,
        mesh=mesh,
        in_specs=placed,
        out_specs=(P("real", "site"), P("real", "site"), P("real")),
        check_vma=False,
    )
```

profile of v0, /device:TPU:0, one launch (start us, length us, event | category | flops | bytes accessed | tf_op | source)
XLA Modules:
  0.0 375.5 jit_solution(16030790064351147388)
XLA Ops:
  7.2 0.0 copy-start
  7.2 0.0 copy-start.8
  7.2 0.9 copy.84
  8.1 0.7 compare_and_fusion.1
  8.8 0.3 copy.54
  9.2 4.2 %gather_fusion.1 = f32[2560,16]{1,0:T(8,128)S(1)} fusion(f32[16,2048]{0,1:T(8,128)S(1)} %copy.54, s32[3072]{0:T(1024)S(1)} %pad_clamp_fusion), kind=kCustom, calls=%fused_computation.1 | custom fusion | bytes 337920 | tf_op jit(solution)/shard_map/jit(_take)/gather | solution.py:34
  13.3 0.0 copy-done.8
  13.3 1.8 subtract_bitcast_fusion
  15.1 0.4 copy.55
  15.5 19.6 %all_gather.7 = f32[64,2560]{1,0:T(8,128)S(1)} all-gather(f32[16,2560]{1,0:T(8,128)S(1)} %copy.55), channel_id=1, replica_groups=mesh['site'=8,'real'=4] {'real'}, dimensions={0}, use_global_device_ids=true | all-gather | bytes 819200 | tf_op jit(solution)/shard_map/all_gather | solution.py:37
  35.1 36.5 %fusion.17 = f32[64,5120]{1,0:T(8,128)S(1)} fusion(f32[64,2560]{1,0:T(8,128)S(1)} %all_gather.7, f32[2560,5120]{1,0:T(8,128)} %param.19), kind=kOutput, calls=%fused_computation.42 | convolution fusion | flops 10066329600 | bytes 54394880 | tf_op jit(solution)/shard_map/dot_general | solution.py:36
  71.6 0.0 copy-start.3
  71.6 51.6 %all-reduce.1 = bf16[64,5120]{1,0:T(8,128)(2,1)} all-reduce(f32[64,5120]{1,0:T(8,128)S(1)} %fusion.17), channel_id=1, replica_groups=mesh['site'=8,'real'=4] {'site'}, use_global_device_ids=true, to_apply=%region_0.1 | all-reduce | flops 327680 | bytes 1966080 | tf_op jit(solution)/shard_map/psum | solution.py:44
  123.2 3.9 %all-to-all-start = ((bf16[4,16,5120]{2,1,0:T(8,128)(2,1)}), bf16[4,16,5120]{2,1,0:T(8,128)(2,1)S(1)}, u32[]{:S(2)}, u32[]{:S(2)}) async-start(bf16[4,16,5120]{2,1,0:T(8,128)(2,1)} %bitcast.7), calls=%async_computation | async-start | bytes 1310720 | tf_op jit(solution)/shard_map/all_to_all | solution.py:45
  127.2 0.4 copy.53
  127.5 4.2 %gather_fusion = f32[2560,2]{1,0:T(8,128)S(1)} fusion(f32[2,2048]{0,1:T(8,128)S(1)} %copy.53, s32[3072]{0:T(1024)S(1)} %pad_clamp_fusion), kind=kCustom, calls=%fused_computation | custom fusion | bytes 51200 | tf_op jit(solution)/shard_map/jit(_take)/gather | solution.py:42
  131.7 1.4 select_bitcast_fusion.1
  133.1 51.1 %all_gather.6 = f32[2,20480]{0,1:T(8,128)} all-gather(f32[2,2560]{0,1:T(8,128)S(1)} %select_bitcast_fusion.1), channel_id=1, replica_groups=mesh['site'=8,'real'=4] {'site'}, dimensions={1}, use_global_device_ids=true | all-gather | bytes 184320 | tf_op jit(solution)/shard_map/all_gather | solution.py:48
  184.2 6.0 %copy.57 = f32[2,20480]{1,0:T(2,128)S(1)} copy(f32[2,20480]{0,1:T(8,128)} %all_gather.6) | data formatting | bytes 327680 | tf_op jit(solution)/shard_map/while | solution.py:64
  190.3 0.3 fusion.9
  190.7 0.3 fusion.8
  191.0 0.3 convolution_bitcast_fusion
  191.3 0.0 all-to-all-done
  191.4 0.0 copy-start.9
  191.4 87.1 %while.24 = (s32[]{:T(128)}, f32[16,2048]{1,0:T(8,128)S(1)}, f32[2,2048]{1,0:T(2,128)S(1)}, f32[2,20480]{1,0:T(2,128)S(1)}, bf16[16,20480]{1,0:T(8,128)(2,1)S(1)...) while((s32[]{:T(128)}, f32[16,2048]{1,0:T(8,128)S(1)}, f32[2,2048]{1,0:T(2,128)S(1)}, ...), condition=%wide.region_2.3_spmd, body=%wide.region_1.2_spmd.sunk | while | flops 209719296 | bytes 1218715 | solution.py:64
  191.6 0.1 fusion.29
  191.8 10.7 %fusion.31 = f32[16,2048]{1,0:T(8,128)S(1)} fusion(f32[16,2048]{1,0:T(8,128)S(1)} %get-tuple-element.281, s32[]{:T(128)S(6)} %select_n.57, bf16[16,20480]{1,0:T(8,128)(2,1)S(1)} %get-tuple-element.293, f32[20480]{0:T(1024)S(1)} %bitcast.59, f32[256]{0:T(256)S(1)} %bitcast.64, f32[20480]{0:T(1024)S(1)} %bitcast.58, f32[256]{0:T(256)S(1)} %bitcast.65), kind=kOutput, calls=%fused_computation.7.clone.1 | convolution fusion | flops 209719296 | bytes 854020 | tf_op jit(solution)/shard_map/while/body/eval_jaxpr/dot_general | solution.py:58
  202.5 0.1 fusion.29
  202.6 10.7 %fusion.31 = f32[16,2048]{1,0:T(8,128)S(1)} fusion(f32[16,2048]{1,0:T(8,128)S(1)} %get-tuple-element.281, s32[]{:T(128)S(6)} %select_n.57, bf16[16,20480]{1,0:T(8,128)(2,1)S(1)} %get-tuple-element.293, f32[20480]{0:T(1024)S(1)} %bitcast.59, f32[256]{0:T(256)S(1)} %bitcast.64, f32[20480]{0:T(1024)S(1)} %bitcast.58, f32[256]{0:T(256)S(1)} %bitcast.65), kind=kOutput, calls=%fused_computation.7.clone.1 | convolution fusion | flops 209719296 | bytes 854020 | tf_op jit(solution)/shard_map/while/body/eval_jaxpr/dot_general | solution.py:58
  213.3 0.1 fusion.29
  213.5 10.7 %fusion.31 = f32[16,2048]{1,0:T(8,128)S(1)} fusion(f32[16,2048]{1,0:T(8,128)S(1)} %get-tuple-element.281, s32[]{:T(128)S(6)} %select_n.57, bf16[16,20480]{1,0:T(8,128)(2,1)S(1)} %get-tuple-element.293, f32[20480]{0:T(1024)S(1)} %bitcast.59, f32[256]{0:T(256)S(1)} %bitcast.64, f32[20480]{0:T(1024)S(1)} %bitcast.58, f32[256]{0:T(256)S(1)} %bitcast.65), kind=kOutput, calls=%fused_computation.7.clone.1 | convolution fusion | flops 209719296 | bytes 854020 | tf_op jit(solution)/shard_map/while/body/eval_jaxpr/dot_general | solution.py:58
  224.2 0.1 fusion.29
  224.4 10.7 %fusion.31 = f32[16,2048]{1,0:T(8,128)S(1)} fusion(f32[16,2048]{1,0:T(8,128)S(1)} %get-tuple-element.281, s32[]{:T(128)S(6)} %select_n.57, bf16[16,20480]{1,0:T(8,128)(2,1)S(1)} %get-tuple-element.293, f32[20480]{0:T(1024)S(1)} %bitcast.59, f32[256]{0:T(256)S(1)} %bitcast.64, f32[20480]{0:T(1024)S(1)} %bitcast.58, f32[256]{0:T(256)S(1)} %bitcast.65), kind=kOutput, calls=%fused_computation.7.clone.1 | convolution fusion | flops 209719296 | bytes 854020 | tf_op jit(solution)/shard_map/while/body/eval_jaxpr/dot_general | solution.py:58
  235.0 0.1 fusion.29
  235.2 10.7 %fusion.31 = f32[16,2048]{1,0:T(8,128)S(1)} fusion(f32[16,2048]{1,0:T(8,128)S(1)} %get-tuple-element.281, s32[]{:T(128)S(6)} %select_n.57, bf16[16,20480]{1,0:T(8,128)(2,1)S(1)} %get-tuple-element.293, f32[20480]{0:T(1024)S(1)} %bitcast.59, f32[256]{0:T(256)S(1)} %bitcast.64, f32[20480]{0:T(1024)S(1)} %bitcast.58, f32[256]{0:T(256)S(1)} %bitcast.65), kind=kOutput, calls=%fused_computation.7.clone.1 | convolution fusion | flops 209719296 | bytes 854020 | tf_op jit(solution)/shard_map/while/body/eval_jaxpr/dot_general | solution.py:58
  245.9 0.1 fusion.29
  246.1 10.7 %fusion.31 = f32[16,2048]{1,0:T(8,128)S(1)} fusion(f32[16,2048]{1,0:T(8,128)S(1)} %get-tuple-element.281, s32[]{:T(128)S(6)} %select_n.57, bf16[16,20480]{1,0:T(8,128)(2,1)S(1)} %get-tuple-element.293, f32[20480]{0:T(1024)S(1)} %bitcast.59, f32[256]{0:T(256)S(1)} %bitcast.64, f32[20480]{0:T(1024)S(1)} %bitcast.58, f32[256]{0:T(256)S(1)} %bitcast.65), kind=kOutput, calls=%fused_computation.7.clone.1 | convolution fusion | flops 209719296 | bytes 854020 | tf_op jit(solution)/shard_map/while/body/eval_jaxpr/dot_general | solution.py:58
  256.8 0.1 fusion.29
  257.0 10.7 %fusion.31 = f32[16,2048]{1,0:T(8,128)S(1)} fusion(f32[16,2048]{1,0:T(8,128)S(1)} %get-tuple-element.281, s32[]{:T(128)S(6)} %select_n.57, bf16[16,20480]{1,0:T(8,128)(2,1)S(1)} %get-tuple-element.293, f32[20480]{0:T(1024)S(1)} %bitcast.59, f32[256]{0:T(256)S(1)} %bitcast.64, f32[20480]{0:T(1024)S(1)} %bitcast.58, f32[256]{0:T(256)S(1)} %bitcast.65), kind=kOutput, calls=%fused_computation.7.clone.1 | convolution fusion | flops 209719296 | bytes 854020 | tf_op jit(solution)/shard_map/while/body/eval_jaxpr/dot_general | solution.py:58
  267.6 0.1 fusion.29
  267.8 10.7 %fusion.31 = f32[16,2048]{1,0:T(8,128)S(1)} fusion(f32[16,2048]{1,0:T(8,128)S(1)} %get-tuple-element.281, s32[]{:T(128)S(6)} %select_n.57, bf16[16,20480]{1,0:T(8,128)(2,1)S(1)} %get-tuple-element.293, f32[20480]{0:T(1024)S(1)} %bitcast.59, f32[256]{0:T(256)S(1)} %bitcast.64, f32[20480]{0:T(1024)S(1)} %bitcast.58, f32[256]{0:T(256)S(1)} %bitcast.65), kind=kOutput, calls=%fused_computation.7.clone.1 | convolution fusion | flops 209719296 | bytes 854020 | tf_op jit(solution)/shard_map/while/body/eval_jaxpr/dot_general | solution.py:58
  278.5 0.0 copy-done.9
  278.5 0.3 copy.58
  278.9 14.1 %gather_fusion.2 = f32[4096,16]{1,0:T(8,128)} fusion(f32[16,2048]{0,1:T(8,128)S(1)} %copy.58, s32[4096]{0:T(1024)S(1)} %fusion.13), kind=kCustom, calls=%fused_computation.2 | custom fusion | bytes 540672 | tf_op jit(solution)/shard_map/jit(_take)/gather | solution.py:67
  293.0 3.6 select_bitcast_fusion
  296.6 0.6 copy.59
  297.2 0.3 multiply_reduce_fusion
  297.4 0.2 copy.63
  297.6 22.7 %while.25 = (s32[]{:T(128)}, f32[16,4096]{1,0:T(8,128)S(1)}, f32[8,16,512]{2,0,1:T(8,128)S(1)}, s32[8,512]{1,0:T(8,128)S(1)}, s32[]{:T(128)}, /*index=5*/s32[]{:T(128)}) while((s32[]{:T(128)}, f32[16,4096]{1,0:T(8,128)S(1)}, f32[8,16,512]{2,0,1:T(8,128)S(1)}, s32[8,512]{1,0:T(8,128)S(1)}, s32[]{:T(128)}, /*index=5*/s32[]{:T(128)}) %tuple.76), condition=%wide.region_5.6_spmd.clone, body=%wide.region_4.5_spmd.clone.sunk | while | flops 404881408 | bytes 628831 | solution.py:115
  297.7 2.8 fusion.32
  300.5 2.8 fusion.32
  303.4 2.8 fusion.32
  306.2 2.8 fusion.32
  309.1 2.8 fusion.32
  311.9 2.8 fusion.32
  314.7 2.8 fusion.32
  317.6 2.8 fusion.32
  320.3 0.0 copy-start.1
  320.4 0.7 copy-done.4
  321.0 0.0 reduce-scatter.2.cloned.1.call-update
  321.1 34.0 %reduce-scatter.2.cloned.1.call-done = f32[16,512]{1,0:T(8,128)} async-done(((f32[16,4096]{1,0:T(8,128)}), f32[16,512]{1,0:T(8,128)}) %reduce-scatter.2.cloned.1.call-update) | async-done | bytes 32784 | tf_op jit(solution)/shard_map/reduce_scatter | solution.py:119
  355.1 0.9 reduce_sum.22
  356.0 12.2 %psum.15 = f32[16]{0:T(128)S(1)} all-reduce(f32[16]{0:T(128)S(1)} %reduce_sum.22), channel_id=1, replica_groups=mesh['site'=8,'real'=4] {'site'}, use_global_device_ids=true, to_apply=%region_8.9 | all-reduce | flops 16 | bytes 128 | tf_op jit(solution)/shard_map/psum | solution.py:120
  368.2 0.5 broadcast_multiply_fusion
  (60 shorter events, 0.6 us)
Async XLA Ops:
  7.2 183.5 %copy-start = (f32[4,36]{1,0:T(4,128)S(1)}, f32[4,36]{1,0:T(4,128)}, u32[]{:S(2)}) copy-start(f32[4,36]{1,0:T(4,128)} %param.29) | copy-start | bytes 1732
  7.2 6.1 %copy-start.8 = (f32[2560]{0:T(1024)S(1)}, f32[2560]{0:T(1024)}, u32[]{:S(2)}) copy-start(f32[2560]{0:T(1024)} %param.18) | copy-start | bytes 30724
  71.6 55.6 %copy-start.3 = (f32[2,2048]{1,0:T(2,128)S(1)}, f32[2,2048]{1,0:T(2,128)}, u32[]{:S(2)}) copy-start(f32[2,2048]{1,0:T(2,128)} %param.20) | copy-start | bytes 49156
  123.2 68.1 %all-to-all-start = ((bf16[4,16,5120]{2,1,0:T(8,128)(2,1)}), bf16[4,16,5120]{2,1,0:T(8,128)(2,1)S(1)}, u32[]{:S(2)}, u32[]{:S(2)}) async-start(bf16[4,16,5120]{2,1,0:T(8,128)(2,1)} %bitcast.7), calls=%async_computation | async-start | bytes 1310720 | tf_op jit(solution)/shard_map/all_to_all | solution.py:45
  127.2 5.9 %copy-start.5 = (s32[4096]{0:T(1024)S(1)}, s32[4096]{0:T(1024)}, u32[]{:S(2)}) copy-start(s32[4096]{0:T(1024)} %param.23) | copy-start | bytes 49156
  127.2 227.9 %reduce-scatter.2.cloned.1.call-start = ((), (), s32[]{:S(2)}) async-start(), calls=%async_computation.2 | async-start | bytes 294912 | tf_op jit(solution)/shard_map/reduce_scatter | solution.py:119
  184.2 6.1 %copy-start.6 = (f32[4096]{0:T(1024)S(1)}, f32[4096]{0:T(1024)}, u32[]{:S(2)}) copy-start(f32[4096]{0:T(1024)} %param.26) | copy-start | bytes 49156
  184.2 6.1 %copy-start.7 = (s32[4096]{0:T(1024)S(1)}, s32[4096]{0:T(1024)}, u32[]{:S(2)}) copy-start(s32[4096]{0:T(1024)} %param.25) | copy-start | bytes 49156
  184.2 6.1 %copy-start.10 = (s32[4096]{0:T(1024)S(1)}, s32[4096]{0:T(1024)}, u32[]{:S(2)}) copy-start(s32[4096]{0:T(1024)} %param.24) | copy-start | bytes 49156
  184.2 6.1 %copy-start.12 = (f32[36]{0:T(128)S(1)}, f32[36]{0:T(128)}, u32[]{:S(2)}) copy-start(f32[36]{0:T(128)} %param.28) | copy-start | bytes 436
  184.2 6.8 %copy-start.11 = (f32[4,36]{1,0:T(4,128)S(1)}, f32[4,36]{1,0:T(4,128)}, u32[]{:S(2)}) copy-start(f32[4,36]{1,0:T(4,128)} %param.27) | copy-start | bytes 1732
  191.4 87.1 %copy-start.9 = (f32[2048]{0:T(1024)S(1)}, f32[2048]{0:T(1024)}, u32[]{:S(2)}) copy-start(f32[2048]{0:T(1024)} %param.22) | copy-start | bytes 24580
  278.5 18.1 %copy-start.2 = (f32[16,2048]{1,0:T(8,128)}, f32[16,2048]{1,0:T(8,128)S(1)}, u32[]{:S(2)}) copy-start(f32[16,2048]{1,0:T(8,128)S(1)} %get-tuple-element.116) | copy-start | bytes 393220
  320.3 0.7 copy-start.4
  320.3 48.4 %copy-start.1 = (f32[4,36]{1,0:T(4,128)S(1)}, f32[4,36]{1,0:T(4,128)}, u32[]{:S(2)}) copy-start(f32[4,36]{1,0:T(4,128)} %param.29) | copy-start | bytes 1732
Sparse Core Ops, SparseCore 0:
  321.2 33.8 reduce-scatter.1
where the time goes:
time: 376 us
  matrix products  145 us (39%)
  blocking collectives  135 us (36%)
  waiting for transfers between devices  34 us (9%)
  local copies, waits for them, and re-layouts  33.8 us (9%)
  between operations  14.3 us (4%)
  other arithmetic  9.19 us (2%)
  starting transfers between devices  3.94 us (1%)
    dot_general x8, matrix products, one_block(): lax.dot_general(weights, cross, (((1,), (1,)), ((), ())), preferred_eleme...  85.4 us
    psum x1, blocking collectives, shards(): summed = lax.psum(partial_w, 'site')  51.6 us
    all_gather x1, blocking collectives, shards(): piece = lax.all_gather(station_xy, 'site', axis=1, tiled=True)  51.1 us
    dot_general x1, matrix products, shards(): jnp.dot(lax.all_gather(innov, 'real', axis=0, tiled=True), inv_cov, preci...  36.5 us
    reduce_scatter x1, waiting for transfers between devices, shards(): lax.psum_scatter(tract_part, 'site', scatter_dimension=1, tiled=True)  34 us
    dot_general x8, matrix products, add_group(): jnp.dot(loss_part, table, precision=lax.Precision.HIGHEST, preferred_elem...  22.2 us
    all_gather x1, blocking collectives, shards(): lax.all_gather(innov, 'real', axis=0, tiled=True)  19.6 us
    gather x1, local copies, waits for them, and re-layouts, shards(): build_im = jnp.take(ln_im, build_local, axis=1)  14.1 us
  transfers between devices with their start and end apart: 2, of which 1 were waited for; matrix products, arithmetic and copies ran while one was open for 3% of the time, Pallas kernels for 0%

commit v1 on v0

--- a/solution.py
+++ b/solution.py
@@ -1,10 +1,33 @@
+import functools
 import math
 import jax
 import jax.numpy as jnp
 from jax import lax
 from jax.sharding import PartitionSpec as P
+from jax.lax import axis_index, axis_size, ppermute
 
 TRACT_DEV = 512
+
+
+def _show_waves(packet, row_dim):
+    shares = axis_size("site")
+    z_new = range(shares)
+    tall = map(lambda i: (i, (i + 1) % shares), z_new)
+    lanes = list(tall)
+
+    def settle_the_spots(reply):
+        if len(reply) == shares:
+            return reply
+        taken_in = ppermute(reply[0], "site", lanes)
+        return settle_the_spots([taken_in, *reply])
+
+    finding = settle_the_spots([packet])
+    block_next = jnp.concatenate(finding, axis=row_dim)
+    q_next = axis_index("site")
+    return jnp.roll(block_next, (q_next + 1) * packet.shape[row_dim], axis=row_dim)
+
+
+edit_the_numbers = functools.partial(_show_waves, row_dim=1)
 
 
 def normal_cdf(value):
@@ -45,7 +68,7 @@
     weights = lax.all_to_all(
         summed.astype(jnp.bfloat16), "real", split_axis=0, concat_axis=1, tiled=True
     )
-    piece = lax.all_gather(station_xy, "site", axis=1, tiled=True)
+    piece = edit_the_numbers(station_xy)
 
     def one_block(index, acc):
         anchor = index * block_width

time: 376 us -> 340 us (0.904)
  blocking collectives: 135 us -> 83.4 us
  waiting for transfers between devices: 34 us -> 53.2 us
  local copies, waits for them, and re-layouts: 33.8 us -> 29.4 us
    all_gather x1 -> x0, blocking collectives: 51.1 us -> none  [shards(): piece = lax.all_gather(station_xy, 'site', axis=1, tiled=True)]
    ppermute x0 -> x7, waiting for transfers between devices: none -> 19.4 us  [settle_the_spots(): taken_in = ppermute(reply[0], 'site', lanes)]
    while x1 -> x0, local copies, waits for them, and re-layouts: 6.04 us -> none  [shards(): cond_field = lax.fori_loop(0, site_block // block_width, one_block, field)]
  transfers between devices with their start and end apart: 2 -> 9, of which waited for: 1 -> 6; matrix products, arithmetic and copies ran while one was open for 3% -> 13% of each run, Pallas kernels for 0% -> 0%
where the time goes in v1:
time: 340 us
  matrix products  145 us (43%)
  blocking collectives  83.4 us (25%)
  waiting for transfers between devices  53.2 us (16%)
  local copies, waits for them, and re-layouts  29.4 us (9%)
  between operations  14.4 us (4%)
  other arithmetic  9.19 us (3%)
  starting transfers between devices  4.68 us (1%)
    dot_general x8, matrix products, one_block(): lax.dot_general(weights, cross, (((1,), (1,)), ((), ())), preferred_eleme...  85.4 us
    psum x1, blocking collectives, shards(): summed = lax.psum(partial_w, 'site')  52.1 us
    dot_general x1, matrix products, shards(): jnp.dot(lax.all_gather(innov, 'real', axis=0, tiled=True), inv_cov, preci...  36.4 us
    reduce_scatter x1, waiting for transfers between devices, shards(): lax.psum_scatter(tract_part, 'site', scatter_dimension=1, tiled=True)  33.8 us
    dot_general x8, matrix products, add_group(): jnp.dot(loss_part, table, precision=lax.Precision.HIGHEST, preferred_elem...  22.2 us
    ppermute x7, waiting for transfers between devices, settle_the_spots(): taken_in = ppermute(reply[0], 'site', lanes)  19.4 us
    all_gather x1, blocking collectives, shards(): lax.all_gather(innov, 'real', axis=0, tiled=True)  19.1 us
    gather x1, local copies, waits for them, and re-layouts, shards(): build_im = jnp.take(ln_im, build_local, axis=1)  14.2 us
  transfers between devices with their start and end apart: 9, of which 6 were waited for; matrix products, arithmetic and copies ran while one was open for 13% of the time, Pallas kernels for 0%

profile of v1, /device:TPU:0, one launch (start us, length us, event | category | flops | bytes accessed | tf_op | source)
XLA Modules:
  0.0 339.9 jit_solution(6694586034641494480)
XLA Ops:
  7.2 0.9 copy.105
  8.1 0.7 compare_and_fusion.1
  8.8 1.1 copy.57
  9.9 4.1 %gather_fusion = f32[2560,2]{1,0:T(8,128)S(1)} fusion(f32[2,2048]{0,1:T(8,128)S(1)} %copy.57, s32[3072]{0:T(1024)S(1)} %pad_clamp_fusion), kind=kCustom, calls=%fused_computation | custom fusion | bytes 51200 | tf_op jit(solution)/shard_map/jit(_take)/gather | solution.py:65
  14.1 1.4 select_bitcast_fusion.1
  15.4 0.4 copy.58
  15.8 0.5 collective-permute-start
  16.3 0.3 copy.61
  16.6 4.1 %gather_fusion.1 = f32[2560,16]{1,0:T(8,128)S(1)} fusion(f32[16,2048]{0,1:T(8,128)S(1)} %copy.61, s32[3072]{0:T(1024)S(1)} %pad_clamp_fusion), kind=kCustom, calls=%fused_computation.1 | custom fusion | bytes 337920 | tf_op jit(solution)/shard_map/jit(_take)/gather | solution.py:57
  20.8 1.8 subtract_bitcast_fusion
  22.6 0.4 copy.62
  23.0 19.1 %all_gather.3 = f32[64,2560]{1,0:T(8,128)S(1)} all-gather(f32[16,2560]{1,0:T(8,128)S(1)} %copy.62), channel_id=1, replica_groups=mesh['site'=8,'real'=4] {'real'}, dimensions={0}, use_global_device_ids=true | all-gather | bytes 819200 | tf_op jit(solution)/shard_map/all_gather | solution.py:60
  42.0 36.4 %fusion.17 = f32[64,5120]{1,0:T(8,128)S(1)} fusion(f32[64,2560]{1,0:T(8,128)S(1)} %all_gather.3, f32[2560,5120]{1,0:T(8,128)} %param.19), kind=kOutput, calls=%fused_computation.59 | convolution fusion | flops 10066329600 | bytes 54394880 | tf_op jit(solution)/shard_map/dot_general | solution.py:59
  78.6 0.2 collective-permute-start.1
  78.7 52.1 %all-reduce.1 = bf16[64,5120]{1,0:T(8,128)(2,1)} all-reduce(f32[64,5120]{1,0:T(8,128)S(1)} %fusion.17), channel_id=1, replica_groups=mesh['site'=8,'real'=4] {'site'}, use_global_device_ids=true, to_apply=%region_0.1 | all-reduce | flops 327680 | bytes 1966080 | tf_op jit(solution)/shard_map/psum | solution.py:67
  130.9 4.0 %all-to-all-start = ((bf16[4,16,5120]{2,1,0:T(8,128)(2,1)}), bf16[4,16,5120]{2,1,0:T(8,128)(2,1)S(1)}, u32[]{:S(2)}, u32[]{:S(2)}) async-start(bf16[4,16,5120]{2,1,0:T(8,128)(2,1)} %bitcast.7), calls=%async_computation | async-start | bytes 1310720 | tf_op jit(solution)/shard_map/all_to_all | solution.py:68
  134.8 0.1 collective-permute-start.2
  134.9 0.3 convolution_bitcast_fusion
  135.2 3.7 %collective-permute-done.2 = f32[2,2560]{1,0:T(2,128)S(1)} collective-permute-done((f32[2,2560]{1,0:T(2,128)S(1)}, f32[2,2560]{1,0:T(2,128)S(1)}, u32[]{:S(2)}, u32[]{:S(2)}) %collective-permute-start.2) | collective-permute-done | bytes 20512 | tf_op jit(solution)/shard_map/ppermute | solution.py:21
  139.0 0.3 fusion.8
  139.3 3.8 %collective-permute-done.3 = f32[2,2560]{1,0:T(2,128)S(1)} collective-permute-done((f32[2,2560]{1,0:T(2,128)S(1)}, f32[2,2560]{1,0:T(2,128)S(1)}, u32[]{:S(2)}, u32[]{:S(2)}) %collective-permute-start.3) | collective-permute-done | bytes 20512 | tf_op jit(solution)/shard_map/ppermute | solution.py:21
  143.1 0.3 fusion.9
  143.4 3.8 %collective-permute-done.4 = f32[2,2560]{1,0:T(2,128)S(1)} collective-permute-done((f32[2,2560]{1,0:T(2,128)S(1)}, f32[2,2560]{1,0:T(2,128)S(1)}, u32[]{:S(2)}, u32[]{:S(2)}) %collective-permute-start.4) | collective-permute-done | bytes 20512 | tf_op jit(solution)/shard_map/ppermute | solution.py:21
  147.2 4.1 %collective-permute-done.5 = f32[2,2560]{1,0:T(2,128)S(1)} collective-permute-done((f32[2,2560]{1,0:T(2,128)S(1)}, f32[2,2560]{1,0:T(2,128)S(1)}, u32[]{:S(2)}, u32[]{:S(2)}) %collective-permute-start.5) | collective-permute-done | bytes 20512 | tf_op jit(solution)/shard_map/ppermute | solution.py:21
  151.4 4.0 %collective-permute-done.6 = f32[2,2560]{1,0:T(2,128)S(1)} collective-permute-done((f32[2,2560]{1,0:T(2,128)S(1)}, f32[2,2560]{1,0:T(2,128)S(1)}, u32[]{:S(2)}, u32[]{:S(2)}) %collective-permute-start.6) | collective-permute-done | bytes 20512 | tf_op jit(solution)/shard_map/ppermute | solution.py:21
  155.6 0.2 constant_dynamic-slice_fusion.4
  156.0 87.1 %while.24 = (s32[]{:T(128)}, f32[16,2048]{1,0:T(8,128)S(1)}, f32[2,2048]{1,0:T(2,128)S(1)}, f32[2,20480]{1,0:T(2,128)S(1)}, bf16[16,20480]{1,0:T(8,128)(2,1)S(1)...) while((s32[]{:T(128)}, f32[16,2048]{1,0:T(8,128)S(1)}, f32[2,2048]{1,0:T(2,128)S(1)}, ...), condition=%wide.region_2.3_spmd, body=%wide.region_1.2_spmd.sunk | while | flops 209719296 | bytes 1218707 | solution.py:87
  156.2 0.1 fusion.29
  156.3 10.7 %fusion.31 = f32[16,2048]{1,0:T(8,128)S(1)} fusion(f32[16,2048]{1,0:T(8,128)S(1)} %get-tuple-element.266, s32[]{:T(128)S(6)} %select_n.72, bf16[16,20480]{1,0:T(8,128)(2,1)S(1)} %get-tuple-element.278, f32[20480]{0:T(1024)S(1)} %bitcast.59, f32[256]{0:T(256)S(1)} %bitcast.64, f32[20480]{0:T(1024)S(1)} %bitcast.58, f32[256]{0:T(256)S(1)} %bitcast.65), kind=kOutput, calls=%fused_computation.7.clone.1 | convolution fusion | flops 209719296 | bytes 854020 | tf_op jit(solution)/shard_map/while/body/eval_jaxpr/dot_general | solution.py:81
  167.1 0.1 fusion.29
  167.2 10.7 %fusion.31 = f32[16,2048]{1,0:T(8,128)S(1)} fusion(f32[16,2048]{1,0:T(8,128)S(1)} %get-tuple-element.266, s32[]{:T(128)S(6)} %select_n.72, bf16[16,20480]{1,0:T(8,128)(2,1)S(1)} %get-tuple-element.278, f32[20480]{0:T(1024)S(1)} %bitcast.59, f32[256]{0:T(256)S(1)} %bitcast.64, f32[20480]{0:T(1024)S(1)} %bitcast.58, f32[256]{0:T(256)S(1)} %bitcast.65), kind=kOutput, calls=%fused_computation.7.clone.1 | convolution fusion | flops 209719296 | bytes 854020 | tf_op jit(solution)/shard_map/while/body/eval_jaxpr/dot_general | solution.py:81
  177.9 0.1 fusion.29
  178.1 10.7 %fusion.31 = f32[16,2048]{1,0:T(8,128)S(1)} fusion(f32[16,2048]{1,0:T(8,128)S(1)} %get-tuple-element.266, s32[]{:T(128)S(6)} %select_n.72, bf16[16,20480]{1,0:T(8,128)(2,1)S(1)} %get-tuple-element.278, f32[20480]{0:T(1024)S(1)} %bitcast.59, f32[256]{0:T(256)S(1)} %bitcast.64, f32[20480]{0:T(1024)S(1)} %bitcast.58, f32[256]{0:T(256)S(1)} %bitcast.65), kind=kOutput, calls=%fused_computation.7.clone.1 | convolution fusion | flops 209719296 | bytes 854020 | tf_op jit(solution)/shard_map/while/body/eval_jaxpr/dot_general | solution.py:81
  188.8 0.1 fusion.29
  188.9 10.7 %fusion.31 = f32[16,2048]{1,0:T(8,128)S(1)} fusion(f32[16,2048]{1,0:T(8,128)S(1)} %get-tuple-element.266, s32[]{:T(128)S(6)} %select_n.72, bf16[16,20480]{1,0:T(8,128)(2,1)S(1)} %get-tuple-element.278, f32[20480]{0:T(1024)S(1)} %bitcast.59, f32[256]{0:T(256)S(1)} %bitcast.64, f32[20480]{0:T(1024)S(1)} %bitcast.58, f32[256]{0:T(256)S(1)} %bitcast.65), kind=kOutput, calls=%fused_computation.7.clone.1 | convolution fusion | flops 209719296 | bytes 854020 | tf_op jit(solution)/shard_map/while/body/eval_jaxpr/dot_general | solution.py:81
  199.6 0.1 fusion.29
  199.8 10.7 %fusion.31 = f32[16,2048]{1,0:T(8,128)S(1)} fusion(f32[16,2048]{1,0:T(8,128)S(1)} %get-tuple-element.266, s32[]{:T(128)S(6)} %select_n.72, bf16[16,20480]{1,0:T(8,128)(2,1)S(1)} %get-tuple-element.278, f32[20480]{0:T(1024)S(1)} %bitcast.59, f32[256]{0:T(256)S(1)} %bitcast.64, f32[20480]{0:T(1024)S(1)} %bitcast.58, f32[256]{0:T(256)S(1)} %bitcast.65), kind=kOutput, calls=%fused_computation.7.clone.1 | convolution fusion | flops 209719296 | bytes 854020 | tf_op jit(solution)/shard_map/while/body/eval_jaxpr/dot_general | solution.py:81
  210.5 0.1 fusion.29
  210.6 10.7 %fusion.31 = f32[16,2048]{1,0:T(8,128)S(1)} fusion(f32[16,2048]{1,0:T(8,128)S(1)} %get-tuple-element.266, s32[]{:T(128)S(6)} %select_n.72, bf16[16,20480]{1,0:T(8,128)(2,1)S(1)} %get-tuple-element.278, f32[20480]{0:T(1024)S(1)} %bitcast.59, f32[256]{0:T(256)S(1)} %bitcast.64, f32[20480]{0:T(1024)S(1)} %bitcast.58, f32[256]{0:T(256)S(1)} %bitcast.65), kind=kOutput, calls=%fused_computation.7.clone.1 | convolution fusion | flops 209719296 | bytes 854020 | tf_op jit(solution)/shard_map/while/body/eval_jaxpr/dot_general | solution.py:81
  221.4 0.1 fusion.29
  221.5 10.7 %fusion.31 = f32[16,2048]{1,0:T(8,128)S(1)} fusion(f32[16,2048]{1,0:T(8,128)S(1)} %get-tuple-element.266, s32[]{:T(128)S(6)} %select_n.72, bf16[16,20480]{1,0:T(8,128)(2,1)S(1)} %get-tuple-element.278, f32[20480]{0:T(1024)S(1)} %bitcast.59, f32[256]{0:T(256)S(1)} %bitcast.64, f32[20480]{0:T(1024)S(1)} %bitcast.58, f32[256]{0:T(256)S(1)} %bitcast.65), kind=kOutput, calls=%fused_computation.7.clone.1 | convolution fusion | flops 209719296 | bytes 854020 | tf_op jit(solution)/shard_map/while/body/eval_jaxpr/dot_general | solution.py:81
  232.2 0.1 fusion.29
  232.4 10.7 %fusion.31 = f32[16,2048]{1,0:T(8,128)S(1)} fusion(f32[16,2048]{1,0:T(8,128)S(1)} %get-tuple-element.266, s32[]{:T(128)S(6)} %select_n.72, bf16[16,20480]{1,0:T(8,128)(2,1)S(1)} %get-tuple-element.278, f32[20480]{0:T(1024)S(1)} %bitcast.59, f32[256]{0:T(256)S(1)} %bitcast.64, f32[20480]{0:T(1024)S(1)} %bitcast.58, f32[256]{0:T(256)S(1)} %bitcast.65), kind=kOutput, calls=%fused_computation.7.clone.1 | convolution fusion | flops 209719296 | bytes 854020 | tf_op jit(solution)/shard_map/while/body/eval_jaxpr/dot_general | solution.py:81
  243.1 0.3 copy.64
  243.4 14.2 %gather_fusion.2 = f32[4096,16]{1,0:T(8,128)} fusion(f32[16,2048]{0,1:T(8,128)S(1)} %copy.64, s32[4096]{0:T(1024)S(1)} %fusion.13), kind=kCustom, calls=%fused_computation.2 | custom fusion | bytes 540672 | tf_op jit(solution)/shard_map/jit(_take)/gather | solution.py:90
  257.6 3.6 %select_bitcast_fusion = f32[16,4096]{0,1:T(8,128)S(1)} fusion(f32[4096,16]{1,0:T(8,128)} %gather_fusion.2, pred[4096]{0:T(1024)(128)(4,1)S(1)} %compare_and_fusion), kind=kLoop, calls=%fused_computation.21 | loop fusion | flops 65536 | bytes 528384 | tf_op jit(solution)/shard_map/jit(_take)/select_n | solution.py:90
  261.2 0.6 copy.65
  261.8 0.3 multiply_reduce_fusion
  262.1 0.2 copy.69
  262.3 22.7 %while.25 = (s32[]{:T(128)}, f32[16,4096]{1,0:T(8,128)S(1)}, f32[8,16,512]{2,0,1:T(8,128)S(1)}, s32[8,512]{1,0:T(8,128)S(1)}, s32[]{:T(128)}, /*index=5*/s32[]{:T(128)}) while((s32[]{:T(128)}, f32[16,4096]{1,0:T(8,128)S(1)}, f32[8,16,512]{2,0,1:T(8,128)S(1)}, s32[8,512]{1,0:T(8,128)S(1)}, s32[]{:T(128)}, /*index=5*/s32[]{:T(128)}) %tuple.73), condition=%wide.region_5.6_spmd.clone, body=%wide.region_4.5_spmd.clone.sunk | while | flops 404881408 | bytes 628823 | solution.py:138
  262.3 2.8 fusion.32
  265.2 2.8 fusion.32
  268.0 2.8 fusion.32
  270.9 2.8 fusion.32
  273.7 2.8 fusion.32
  276.5 2.8 fusion.32
  279.4 2.8 fusion.32
  282.2 2.8 fusion.32
  285.0 0.7 copy-done.4
  285.7 0.0 reduce-scatter.2.cloned.1.call-update
  285.7 33.8 %reduce-scatter.2.cloned.1.call-done = f32[16,512]{1,0:T(8,128)} async-done(((f32[16,4096]{1,0:T(8,128)}), f32[16,512]{1,0:T(8,128)}) %reduce-scatter.2.cloned.1.call-update) | async-done | bytes 32784 | tf_op jit(solution)/shard_map/reduce_scatter | solution.py:142
  319.5 0.9 reduce_sum.22
  320.4 12.2 %psum.15 = f32[16]{0:T(128)S(1)} all-reduce(f32[16]{0:T(128)S(1)} %reduce_sum.22), channel_id=1, replica_groups=mesh['site'=8,'real'=4] {'site'}, use_global_device_ids=true, to_apply=%region_8.9 | all-reduce | flops 16 | bytes 128 | tf_op jit(solution)/shard_map/psum | solution.py:143
  332.6 0.5 broadcast_multiply_fusion
  (90 shorter events, 0.9 us)
Async XLA Ops:
  7.2 127.7 %copy-start = (f32[4,36]{1,0:T(4,128)S(1)}, f32[4,36]{1,0:T(4,128)}, u32[]{:S(2)}) copy-start(f32[4,36]{1,0:T(4,128)} %param.27) | copy-start | bytes 1732
  15.4 5.4 %copy-start.8 = (f32[2560]{0:T(1024)S(1)}, f32[2560]{0:T(1024)}, u32[]{:S(2)}) copy-start(f32[2560]{0:T(1024)} %param.18) | copy-start | bytes 30724
  15.8 62.7 %collective-permute-start = (f32[2,2560]{1,0:T(2,128)S(1)}, f32[2,2560]{1,0:T(2,128)S(1)}, u32[]{:S(2)}, u32[]{:S(2)}) collective-permute-start(f32[2,2560]{1,0:T(2,128)S(1)} %copy.58), channel_id=1, source_target_pairs={{0,4},{4,8},{8,12},{12,16},{16,20},{20,24},{24,28},{28,0},{1,5},{5... | collective-permute-start | bytes 61448 | tf_op jit(solution)/shard_map/ppermute | solution.py:21
  78.5 56.4 %copy-start.10 = (s32[4096]{0:T(1024)S(1)}, s32[4096]{0:T(1024)}, u32[]{:S(2)}) copy-start(s32[4096]{0:T(1024)} %param.24) | copy-start | bytes 49156
  78.5 60.5 %copy-start.11 = (f32[4,36]{1,0:T(4,128)S(1)}, f32[4,36]{1,0:T(4,128)}, u32[]{:S(2)}) copy-start(f32[4,36]{1,0:T(4,128)} %param.29) | copy-start | bytes 1732
  78.5 64.6 %copy-start.12 = (f32[36]{0:T(128)S(1)}, f32[36]{0:T(128)}, u32[]{:S(2)}) copy-start(f32[36]{0:T(128)} %param.28) | copy-start | bytes 436
  78.5 68.7 %copy-start.5 = (s32[4096]{0:T(1024)S(1)}, s32[4096]{0:T(1024)}, u32[]{:S(2)}) copy-start(s32[4096]{0:T(1024)} %param.23) | copy-start | bytes 49156
  78.5 72.8 %copy-start.6 = (f32[4096]{0:T(1024)S(1)}, f32[4096]{0:T(1024)}, u32[]{:S(2)}) copy-start(f32[4096]{0:T(1024)} %param.26) | copy-start | bytes 49156
  78.5 72.8 %copy-start.7 = (s32[4096]{0:T(1024)S(1)}, s32[4096]{0:T(1024)}, u32[]{:S(2)}) copy-start(s32[4096]{0:T(1024)} %param.25) | copy-start | bytes 49156
  78.6 56.3 %collective-permute-start.1 = (f32[2,2560]{1,0:T(2,128)S(1)}, f32[2,2560]{1,0:T(2,128)S(1)}, u32[]{:S(2)}, u32[]{:S(2)}) collective-permute-start(f32[2,2560]{1,0:T(2,128)S(1)} %collective-permute-done), channel_id=1, source_target_pairs={{0,4},{4,8},{8,12},{12,16},{16,20},{20,24},{24,28},{28,0},{1,5},{5... | collective-permute-start | bytes 61448 | tf_op jit(solution)/shard_map/ppermute | solution.py:21
  130.8 25.1 %copy-start.3 = (f32[2,2048]{1,0:T(2,128)S(1)}, f32[2,2048]{1,0:T(2,128)}, u32[]{:S(2)}) copy-start(f32[2,2048]{1,0:T(2,128)} %param.20) | copy-start | bytes 49156
  130.9 25.0 %all-to-all-start = ((bf16[4,16,5120]{2,1,0:T(8,128)(2,1)}), bf16[4,16,5120]{2,1,0:T(8,128)(2,1)S(1)}, u32[]{:S(2)}, u32[]{:S(2)}) async-start(bf16[4,16,5120]{2,1,0:T(8,128)(2,1)} %bitcast.7), calls=%async_computation | async-start | bytes 1310720 | tf_op jit(solution)/shard_map/all_to_all | solution.py:68
  134.8 184.7 %reduce-scatter.2.cloned.1.call-start = ((), (), s32[]{:S(2)}) async-start(), calls=%async_computation.2 | async-start | bytes 294912 | tf_op jit(solution)/shard_map/reduce_scatter | solution.py:142
  134.8 4.2 %collective-permute-start.2 = (f32[2,2560]{1,0:T(2,128)S(1)}, f32[2,2560]{1,0:T(2,128)S(1)}, u32[]{:S(2)}, u32[]{:S(2)}) collective-permute-start(f32[2,2560]{1,0:T(2,128)S(1)} %collective-permute-done.1), channel_id=1, source_target_pairs={{0,4},{4,8},{8,12},{12,16},{16,20},{20,24},{24,28},{28,0},{1,5},{5... | collective-permute-start | bytes 61448 | tf_op jit(solution)/shard_map/ppermute | solution.py:21
  139.0 4.1 %collective-permute-start.3 = (f32[2,2560]{1,0:T(2,128)S(1)}, f32[2,2560]{1,0:T(2,128)S(1)}, u32[]{:S(2)}, u32[]{:S(2)}) collective-permute-start(f32[2,2560]{1,0:T(2,128)S(1)} %collective-permute-done.2), channel_id=1, source_target_pairs={{0,4},{4,8},{8,12},{12,16},{16,20},{20,24},{24,28},{28,0},{1,5},{5... | collective-permute-start | bytes 61448 | tf_op jit(solution)/shard_map/ppermute | solution.py:21
  143.1 4.1 %collective-permute-start.4 = (f32[2,2560]{1,0:T(2,128)S(1)}, f32[2,2560]{1,0:T(2,128)S(1)}, u32[]{:S(2)}, u32[]{:S(2)}) collective-permute-start(f32[2,2560]{1,0:T(2,128)S(1)} %collective-permute-done.3), channel_id=1, source_target_pairs={{0,4},{4,8},{8,12},{12,16},{16,20},{20,24},{24,28},{28,0},{1,5},{5... | collective-permute-start | bytes 61448 | tf_op jit(solution)/shard_map/ppermute | solution.py:21
  147.2 4.1 %collective-permute-start.5 = (f32[2,2560]{1,0:T(2,128)S(1)}, f32[2,2560]{1,0:T(2,128)S(1)}, u32[]{:S(2)}, u32[]{:S(2)}) collective-permute-start(f32[2,2560]{1,0:T(2,128)S(1)} %collective-permute-done.4), channel_id=1, source_target_pairs={{0,4},{4,8},{8,12},{12,16},{16,20},{20,24},{24,28},{28,0},{1,5},{5... | collective-permute-start | bytes 61448 | tf_op jit(solution)/shard_map/ppermute | solution.py:21
  151.3 4.1 %collective-permute-start.6 = (f32[2,2560]{1,0:T(2,128)S(1)}, f32[2,2560]{1,0:T(2,128)S(1)}, u32[]{:S(2)}, u32[]{:S(2)}) collective-permute-start(f32[2,2560]{1,0:T(2,128)S(1)} %collective-permute-done.5), channel_id=1, source_target_pairs={{0,4},{4,8},{8,12},{12,16},{16,20},{20,24},{24,28},{28,0},{1,5},{5... | collective-permute-start | bytes 61448 | tf_op jit(solution)/shard_map/ppermute | solution.py:21
  155.9 87.1 %copy-start.9 = (f32[2048]{0:T(1024)S(1)}, f32[2048]{0:T(1024)}, u32[]{:S(2)}) copy-start(f32[2048]{0:T(1024)} %param.22) | copy-start | bytes 24580
  243.1 18.2 %copy-start.2 = (f32[16,2048]{1,0:T(8,128)}, f32[16,2048]{1,0:T(8,128)S(1)}, u32[]{:S(2)}) copy-start(f32[16,2048]{1,0:T(8,128)S(1)} %get-tuple-element.116) | copy-start | bytes 393220
  285.0 0.7 copy-start.4
  285.0 48.1 %copy-start.1 = (f32[4,36]{1,0:T(4,128)S(1)}, f32[4,36]{1,0:T(4,128)}, u32[]{:S(2)}) copy-start(f32[4,36]{1,0:T(4,128)} %param.27) | copy-start | bytes 1732
Sparse Core Ops, SparseCore 0:
  285.8 33.6 reduce-scatter.1
